TPU v7x, 256 devices: a whole 4x4x8 slice. The times are simulated.
256 devices in a mesh: rep: 32 (over z, y_hi, core), fsdp: 8 (over y_lo, x).
Axes of the slice: x: 4, y: 4 (y_hi: 2, y_lo: 2; y = y_hi * 2 + y_lo), z: 8, core: 2. Of those that a mesh axis runs over, the one named last changes fastest.
Arguments:
- latent_tokens: bfloat16 [32, 4096, 4096], P('rep', 'fsdp'), may hold values from -6 to 6
- actions: int32 [32, 16], P('rep'), may hold values from 0 to 7
- action_table: bfloat16 [8, 4096], replicated, may hold values from -6 to 6
- key_value_weight: bfloat16 [32, 4096, 1024], P('rep', 'fsdp'), may hold values from -0.09375 to 0.09375
- queries: bfloat16 [32, 4096, 2048], P('rep', 'fsdp'), may hold values from -6 to 6
- output_cotangent: bfloat16 [32, 4096, 2048], P('rep', 'fsdp'), may hold values from -0.09375 to 0.09375
- outer_delta: float32 [32, 256, 4096], P('rep', 'fsdp'), may hold values from -6 to 6
- momentum: float32 [256, 4096], P('fsdp'), may hold values from -6 to 6
- anchor: float32 [256, 4096], P('fsdp'), may hold values from -6 to 6
Outputs:
- weight_gradient: bfloat16 [32, 4096, 1024], P('rep', 'fsdp')
- new_momentum: float32 [256, 4096], P('fsdp')
- new_anchor: float32 [256, 4096], P('fsdp')
All inputs are finite; a program needn't handle non-finite values.
Results may differ from a plain program's by a relative error of at most 0.019.
Values may be sent and summed in bfloat16 or wider, within the bound.
A program may use at most 128 MiB of HBM per device.

v0:
```python
import jax
import jax.numpy as jnp
from jax import lax
from jax.sharding import PartitionSpec as P

HEAD_DIM = 128
KV_HEADS = 4
GROUP = 4
ACTIONS = 8
FRAMES = 16


MOMENTUM_RATE = 0.9
OUTER_RATE = 0.7


def condition(latents, frame_actions, action_table):
    token_count = latents.shape[0]
    patch_count = token_count // FRAMES
    one_hot = (frame_actions[:, None] == jnp.arange(ACTIONS, dtype=jnp.int32)[None, :]).astype(
        jnp.bfloat16
    )
    frame_embed = jnp.dot(one_hot, action_table, preferred_element_type=jnp.float32)
    summed = latents.astype(jnp.float32).reshape(patch_count, FRAMES, -1) + frame_embed[None]
    return summed.reshape(token_count, -1).astype(jnp.bfloat16)


def attention_grad(key_value, query_rows, cotangent):
    token_count = query_rows.shape[0]
    patch_count = token_count // FRAMES
    split_at = KV_HEADS * HEAD_DIM
    key_heads = key_value[:, :split_at].reshape(patch_count, FRAMES, KV_HEADS, HEAD_DIM)
    value_heads = key_value[:, split_at:].reshape(patch_count, FRAMES, KV_HEADS, HEAD_DIM)
    query_heads = query_rows.reshape(patch_count, FRAMES, KV_HEADS, GROUP, HEAD_DIM)
    upstream = cotangent.reshape(patch_count, FRAMES, KV_HEADS, GROUP, HEAD_DIM)
    score_scale = HEAD_DIM ** (-0.5)
    scores = (
        jnp.einsum("pfkgd,ptkd->pkgft", query_heads, key_heads, preferred_element_type=jnp.float32)
        * score_scale
    )
    frame_index = jnp.arange(FRAMES, dtype=jnp.int32)
    causal = frame_index[None, :] <= frame_index[:, None]
    exp_scores = jnp.where(causal, jnp.exp(scores), jnp.float32(0.0))
    probabilities = exp_scores / jnp.sum(exp_scores, axis=-1, keepdims=True)
    probs_low = probabilities.astype(jnp.bfloat16)
    prob_grad = jnp.einsum(
        "pfkgd,ptkd->pkgft", upstream, value_heads, preferred_element_type=jnp.float32
    )
    score_grad = probabilities * (
        prob_grad - jnp.sum(probabilities * prob_grad, axis=-1, keepdims=True)
    )
    score_low = score_grad.astype(jnp.bfloat16)
    value_grad = jnp.einsum(
        "pkgft,pfkgd->ptkd", probs_low, upstream, preferred_element_type=jnp.float32
    )
    key_grad = (
        jnp.einsum("pkgft,pfkgd->ptkd", score_low, query_heads, preferred_element_type=jnp.float32)
        * score_scale
    )
    joined = jnp.concatenate(
        [key_grad.reshape(token_count, -1), value_grad.reshape(token_count, -1)], axis=1
    )
    return joined.astype(jnp.bfloat16)


def nesterov(summed, replica_count, momentum_rows, anchor_rows):
    average = summed / replica_count
    momentum_next = MOMENTUM_RATE * momentum_rows + average
    anchor_next = anchor_rows - OUTER_RATE * (average + MOMENTUM_RATE * momentum_next)
    return (momentum_next, anchor_next)


def body(
    latent_tokens,
    actions,
    action_table,
    key_value_weight,
    queries,
    output_cotangent,
    outer_delta,
    momentum,
    anchor,
):
    conditioned = condition(latent_tokens[0], actions[0], action_table)
    weight = key_value_weight[0]
    columns = conditioned
    key_value_sum = jnp.dot(
        columns,
        lax.all_gather(weight, "fsdp", axis=0, tiled=True),
        preferred_element_type=jnp.float32,
    )
    key_value = key_value_sum.astype(jnp.bfloat16)
    key_value_grad = attention_grad(key_value, queries[0], output_cotangent[0])
    columns = conditioned
    gradient = lax.psum_scatter(
        jnp.einsum("td,tk->dk", columns, key_value_grad, preferred_element_type=jnp.float32).astype(
            jnp.bfloat16
        ),
        "fsdp",
        scatter_dimension=0,
        tiled=True,
    )
    weight_gradient = gradient[None]
    replica_delta = outer_delta[0]
    replica_count = lax.axis_size("rep")
    summed = lax.psum(replica_delta.astype(jnp.bfloat16), "rep").astype(jnp.float32)
    new_momentum, new_anchor = nesterov(summed, replica_count, momentum, anchor)
    return (weight_gradient, new_momentum, new_anchor)


def solution(mesh):
    return jax.shard_map(
        body,
        mesh=mesh,
        in_specs=(
            P("rep", "fsdp", None),
            P("rep", None),
            P(),
            P("rep", "fsdp", None),
            P("rep", "fsdp", None),
            P("rep", "fsdp", None),
            P("rep", "fsdp", None),
            P("fsdp", None),
            P("fsdp", None),
        ),
        out_specs=(P("rep", "fsdp", None), P("fsdp", None), P("fsdp", None)),
        check_vma=False,
    )
```

profile of v0, /device:TPU:8, one launch (start us, length us, event | category | flops | bytes accessed | tf_op | source)
XLA Modules:
  0.0 416.0 jit_solution(15211228956480396095)
XLA Ops:
  8.0 0.0 copy-start
  8.0 0.0 copy-start.2
  8.0 0.0 all-gather.3.cloned.1.call-start
  8.1 0.7 all-gather.3.cloned.1.call-update
  8.8 0.0 all-reduce.2.cloned.1.call-start
  8.8 1.8 convert_bitcast_fusion
  10.6 0.0 all-reduce.2.cloned.1.call-update
  10.6 0.0 reduce-scatter.2.cloned.1.call-start
  10.7 0.0 copy-start.7
  10.7 4.4 %reshape_squeeze.6 = bf16[32,16,4,4,128]{4,3,2,1,0:T(4,128)(2,1)} reshape(bf16[1,512,2048]{2,1,0:T(8,128)(2,1)} %param.13) | data formatting | bytes 4194304 | tf_op jit(solution)/shard_map/reshape;squeeze | solution.py:34
  15.1 0.0 copy-done.2
  15.1 2.7 reshape_squeeze.7
  17.9 0.0 copy-done
  17.9 0.0 copy-done.7
  17.9 0.2 fusion.63
  18.1 5.3 %fusion = bf16[512,4096]{1,0:T(8,128)(2,1)} fusion(bf16[1,512,4096]{2,1,0:T(8,128)(2,1)} %param.9, f32[16,4096]{1,0:T(8,128)S(1)} %fusion.63), kind=kLoop, calls=%fused_computation.1 | loop fusion | flops 6291456 | bytes 8650752 | tf_op jit(solution)/shard_map/convert_element_type | solution.py:25
  23.4 84.0 %all-gather.3.cloned.1.call-done = bf16[1,4096,1024]{2,1,0:T(8,128)(2,1)} async-done(((bf16[1,512,1024]{2,1,0:T(8,128)(2,1)}), bf16[1,4096,1024]{2,1,0:T(8,128)(2,1)}) %all-gather.3.cloned.1.call-update) | async-done | bytes 8388624 | tf_op jit(solution)/shard_map/all_gather | solution.py:89
  107.3 9.2 %fusion.19 = bf16[512,1024]{1,0:T(8,128)(2,1)S(1)} fusion(bf16[512,4096]{1,0:T(8,128)(2,1)} %fusion, bf16[1,4096,1024]{2,1,0:T(8,128)(2,1)} %all-gather.3.cloned.1.call-done), kind=kOutput, calls=%fused_computation.23 | convolution fusion | flops 4295491584 | bytes 13631488 | tf_op jit(solution)/shard_map/dot_general | solution.py:87
  116.5 0.0 copy-start.3
  116.5 0.1 fusion.69
  116.6 0.9 reshape.32
  117.5 0.1 reshape.33
  117.7 0.0 copy-start.4
  117.7 0.6 copy-done.3
  118.3 6.2 %fusion.7 = (f32[32,4,4,16]{3,2,1,0:T(4,128)S(1)}, f32[32,4,16,16,4]{3,2,4,1,0:T(8,128)S(1)}) fusion(pred[16,16]{0,1:T(8,128)(4,1)S(1)} %iota_compare_fusion, bf16[32,16,4,4,128]{4,3,2,1,0:T(4,128)(2,1)S(1)} %copy-done.3, bf16[32,16,4,128,1]{3,2,1,0,4:T(4,128)(2,1)} %bitcast.82), kind=kOutput, calls=%fused_computation.12 | convolution fusion | flops 33939456 | bytes 3178752 | tf_op jit(solution)/shard_map/pfkgd,ptkd->pkgft/dot_general | solution.py:38
  124.5 0.0 copy-done.4
  124.5 1.4 fusion.47
  125.9 5.4 %fusion.3 = (f32[32,4,4,16]{3,2,1,0:T(4,128)S(1)}, f32[32,4,16,16,4]{3,2,4,1,0:T(8,128)S(1)}) fusion(f32[32,4,4,16]{3,2,1,0:T(4,128)S(1)} %get-tuple-element.7, f32[32,4,16,16,4]{3,2,4,1,0:T(8,128)S(1)} %get-tuple-element.8, pred[16,16]{0,1:T(8,128)(4,1)S(1)} %iota_compare_fusion, bf16[32,16,4,4,128]{4,3,2,1,0:T(4,128)(2,1)S(1)} %copy-done.4, ...), kind=kOutput, calls=%fused_computation.7 | convolution fusion | flops 34201600 | bytes 3735808 | tf_op jit(solution)/shard_map/pfkgd,ptkd->pkgft/dot_general | solution.py:46
  131.3 1.9 fusion.52
  133.1 0.0 copy-start.1
  133.2 0.2 copy.23
  133.4 0.3 copy.25
  133.7 0.2 copy_bitcast_fusion
  133.8 1.5 copy-done.1
  135.3 7.1 %convolution_convert_fusion = bf16[4096,1024]{1,0:T(8,128)(2,1)} fusion(bf16[512,4096]{1,0:T(8,128)(2,1)S(1)} %copy-done.1, bf16[512,512]{1,0:T(8,128)(2,1)S(1)} %get-tuple-element.11, bf16[512,512]{1,0:T(8,128)(2,1)S(1)} %get-tuple-element.12), kind=kOutput, calls=%fused_computation.4 | convolution fusion | flops 4301258752 | bytes 13631488 | tf_op jit(solution)/shard_map/td,tk->dk/dot_general | solution.py:96
  142.4 0.0 copy-start.5
  142.4 0.0 copy-start.6
  142.4 0.0 reduce-scatter.2.cloned.1.call-update
  142.4 264.1 %all-reduce.2.cloned.1.call-done = bf16[32,4096]{1,0:T(8,128)(2,1)} async-done(((bf16[32,4096]{1,0:T(8,128)(2,1)}), bf16[32,4096]{1,0:T(8,128)(2,1)}) %all-reduce.2.cloned.1.call-update) | async-done | bytes 262160 | tf_op jit(solution)/shard_map/psum | solution.py:106
  406.5 0.0 copy-done.5
  406.5 0.0 copy-done.6
  406.6 2.1 multiply_subtract_fusion
  408.6 0.0 reduce-scatter.2.cloned.1.call-done
  (1 shorter events, 0.0 us)
Async XLA Ops:
  8.0 9.9 %copy-start = (bf16[8,4096]{1,0:T(8,128)(2,1)S(1)}, bf16[8,4096]{1,0:T(8,128)(2,1)}, u32[]{:S(2)}) copy-start(bf16[8,4096]{1,0:T(8,128)(2,1)} %param.11) | copy-start | bytes 196612
  8.0 7.1 %copy-start.2 = (bf16[1,512,2048]{2,1,0:T(8,128)(2,1)S(1)}, bf16[1,512,2048]{2,1,0:T(8,128)(2,1)}, u32[]{:S(2)}) copy-start(bf16[1,512,2048]{2,1,0:T(8,128)(2,1)} %param.14) | copy-start | bytes 6291460
  8.0 99.3 %all-gather.3.cloned.1.call-start = ((), (), s32[]{:S(2)}) async-start(), calls=%async_computation.3 | async-start | bytes 9437184 | tf_op jit(solution)/shard_map/all_gather | solution.py:89
  8.8 397.8 %all-reduce.2.cloned.1.call-start = ((), (), s32[]{:S(2)}) async-start(), calls=%async_computation.2 | async-start | bytes 524288 | tf_op jit(solution)/shard_map/psum | solution.py:106
  10.6 398.0 %reduce-scatter.2.cloned.1.call-start = ((), (), s32[]{:S(2)}) async-start(), calls=%async_computation.1 | async-start | bytes 9437184 | tf_op jit(solution)/shard_map/reduce_scatter | solution.py:95
  10.7 7.2 %copy-start.7 = (s32[1,16]{1,0:T(1,128)S(1)}, s32[1,16]{1,0:T(1,128)}, u32[]{:S(2)}) copy-start(s32[1,16]{1,0:T(1,128)} %param.10) | copy-start | bytes 196
  116.5 1.8 copy-start.3
  117.7 6.8 %copy-start.4 = (bf16[32,16,4,4,128]{4,3,2,1,0:T(4,128)(2,1)S(1)}, bf16[32,16,4,4,128]{4,3,2,1,0:T(4,128)(2,1)}, u32[]{:S(2)}) copy-start(bf16[32,16,4,4,128]{4,3,2,1,0:T(4,128)(2,1)} %reshape_squeeze.7) | copy-start | bytes 6291460
  133.1 2.2 copy-start.1
  142.4 264.1 %copy-start.5 = (f32[32,4096]{1,0:T(8,128)S(1)}, f32[32,4096]{1,0:T(8,128)}, u32[]{:S(2)}) copy-start(f32[32,4096]{1,0:T(8,128)} %param.17) | copy-start | bytes 1572868
  142.4 264.1 %copy-start.6 = (f32[32,4096]{1,0:T(8,128)S(1)}, f32[32,4096]{1,0:T(8,128)}, u32[]{:S(2)}) copy-start(f32[32,4096]{1,0:T(8,128)} %param.16) | copy-start | bytes 1572868
Sparse Core Ops, SparseCore 0:
  10.6 96.6 all-gather.2
  142.6 94.0 reduce-scatter.1
Sparse Core Ops, SparseCore 1:
  12.4 394.1 all-reduce.1
where the time goes:
time: 418 us; the launch traced here: 416 us
  waiting for transfers between devices  349 us (83%)
  matrix products  31.3 us (7%)
  between operations  15.6 us (4%)
  local copies, waits for them, and re-layouts  11.1 us (3%)
  other arithmetic  9.09 us (2%)
    psum x1, waiting for transfers between devices, body(): lax.psum(replica_delta.astype(jnp.bfloat16), 'rep').astype(jnp.float32)  264 us
    all_gather x1, waiting for transfers between devices, body(): lax.all_gather(weight, 'fsdp', axis=0, tiled=True)  84 us
    dot_general x1, matrix products, body(): jnp.dot(columns, lax.all_gather(weight, 'fsdp', axis=0, tiled=True), pref...  9.17 us
  transfers between devices with their start and end apart: 3, of which 2 were waited for; matrix products, arithmetic and copies ran while one was open for 12% of the time, Pallas kernels for 0%

commit v1 on v0

v1 whole, which is shorter than its diff:
```python
import functools

import jax
import jax.numpy as jnp
from jax import lax
from jax.experimental import pallas as pl
from jax.experimental.pallas import tpu as pltpu
from jax.sharding import PartitionSpec as P

MESH = pl.DeviceIdType.MESH
HEAD_DIM = 128
KV_HEADS = 4
GROUP = 4
ACTIONS = 8
FRAMES = 16
MOMENTUM_RATE = 0.9
OUTER_RATE = 0.7

TOK = 512
BLK = 512
HW = 2 * HEAD_DIM
CH = 128
LOG2E = 1.4426950408889634


def ring_index(core, half, pos):
    even = 4 * half + pos
    row = lax.rem(lax.div(pos + 1, 2), 2)
    odd = 4 * row + half + lax.div(pos, 2) * (3 - 2 * half)
    return even + core * (odd - even)


def kernel(
    lat, w, emb, q, cot, delta, mom, anc,
    wg_out, nm_out, na_out,
    X, XT, WG, QV, CV, EM, MK, O, KS, KR, G, S3, S2, S1, T2, T1, G0, OA, OB, RL, RR, OUT,
    DL, CR, AC, R1, R2, R3, R4, FU, MO, AN, NM, NA,
    send, recv, local,
):
    f32, bf16 = jnp.float32, jnp.bfloat16
    rep = lax.axis_index("rep")
    fsdp = lax.axis_index("fsdp")
    core = lax.rem(rep, 2)
    y_hi = lax.rem(lax.div(rep, 2), 2)
    z = lax.div(rep, 4)
    hi, lo = lax.div(fsdp, 4), lax.rem(fsdp, 4)
    u = lax.div(lo, 2)
    half = hi + core * (lo + u * (3 - 2 * lo) - hi)
    pos = lo + core * (hi + u * (3 - 2 * hi) - lo)
    slot_pos = [pos, lax.rem(pos + 3, 4), lax.rem(pos + 1, 4), lax.rem(pos + 2, 4)]
    mine = [ring_index(core, half, s) for s in slot_pos]
    theirs = [ring_index(core, 1 - half, s) for s in slot_pos]
    left, right, partner = {"fsdp": mine[1]}, {"fsdp": mine[2]}, {"fsdp": theirs[0]}

    def rep_peer(z_, y_, c_):
        return {"rep": z_ * 4 + y_ * 2 + c_}

    bit1, bit2, bit4 = lax.rem(z, 2), lax.rem(lax.div(z, 2), 2), lax.div(z, 4)
    sibling = rep_peer(z, y_hi, 1 - core)
    z_one = rep_peer(z + 1 - 2 * bit1, y_hi, core)
    z_two = rep_peer(z + 2 - 4 * bit2, y_hi, core)
    z_four = rep_peer(z + 4 - 8 * bit4, y_hi, core)
    across = rep_peer(z, 1 - y_hi, core)

    counts = {"remote": 0, "local": 0}

    def remote(src, dst, device):
        n = counts["remote"]
        counts["remote"] = n + 1
        return pltpu.make_async_remote_copy(
            src_ref=src, dst_ref=dst, send_sem=send.at[n], recv_sem=recv.at[n],
            device_id=device, device_id_type=MESH,
        )

    def nearby(src, dst):
        n = counts["local"]
        counts["local"] = n + 1
        return pltpu.make_async_copy(src, dst, local.at[n])

    def columns(i):
        return pl.ds(pl.multiple_of(i * BLK, BLK), BLK)

    keys, values = pl.ds(0, HEAD_DIM), pl.ds(HEAD_DIM, HEAD_DIM)
    own, other = pl.ds(0, TOK), pl.ds(TOK, TOK)

    load_w = [
        [
            nearby(w.at[0, :, pl.ds(k * HEAD_DIM, HEAD_DIM)], WG.at[k, 0, :, keys]),
            nearby(w.at[0, :, pl.ds((KV_HEADS + k) * HEAD_DIM, HEAD_DIM)], WG.at[k, 0, :, values]),
        ]
        for k in range(KV_HEADS)
    ]
    load_x = [nearby(lat.at[0, :, columns(mine[s])], X.at[s, own, :]) for s in range(4)]
    load_emb = nearby(emb, EM)
    load_delta = nearby(delta.at[0], DL)
    load_q, load_c = nearby(q.at[0], QV), nearby(cot.at[0], CV)
    load_m, load_a = nearby(mom, MO), nearby(anc, AN)
    for c in load_w[0]:
        c.start()
    load_delta.start()
    load_emb.start()
    for c in load_x:
        c.start()
    for k in range(1, KV_HEADS):
        for c in load_w[k]:
            c.start()
    for c in (load_q, load_c, load_m, load_a):
        c.start()

    lat_send = [
        remote(lat.at[0, :, columns(theirs[s])], X.at[s, other, :], partner) for s in range(4)
    ]
    w_right = [remote(WG.at[k, 0], WG.at[k, 1], right) for k in range(KV_HEADS)]
    w_left = [remote(WG.at[k, 0], WG.at[k, 2], left) for k in range(KV_HEADS)]
    w_right2 = [remote(WG.at[k, 1, :, keys], WG.at[k, 3, :, keys], right) for k in range(KV_HEADS)]
    w_left2 = [remote(WG.at[k, 2, :, values], WG.at[k, 3, :, values], left) for k in range(KV_HEADS)]
    kv_send = [remote(KS.at[k], KR.at[k], partner) for k in range(KV_HEADS)]
    g_send = [remote(G.at[k, own, :], G.at[k, other, :], partner) for k in range(KV_HEADS)]
    opp_right = [remote(S3.at[k, :, keys], OA.at[k], right) for k in range(KV_HEADS)]
    opp_left = [remote(S3.at[k, :, values], OB.at[k], left) for k in range(KV_HEADS)]
    to_right_k = [remote(S2.at[k, :, keys], RL.at[k, :, keys], right) for k in range(KV_HEADS)]
    to_right_v = [remote(S2.at[k, :, values], RL.at[k, :, values], right) for k in range(KV_HEADS)]
    to_left_k = [remote(S1.at[k, :, keys], RR.at[k, :, keys], left) for k in range(KV_HEADS)]
    to_left_v = [remote(S1.at[k, :, values], RR.at[k, :, values], left) for k in range(KV_HEADS)]

    rows_mine = pl.ds(pl.multiple_of(core * 16, 16), 16)
    rows_other = pl.ds(pl.multiple_of((1 - core) * 16, 16), 16)

    def cols_at(start, width):
        return pl.ds(pl.multiple_of(start, 256), width)

    c1 = bit1 * 2048
    c2 = c1 + bit2 * 1024
    c4 = c2 + bit4 * 512
    cy = c4 + y_hi * 256
    o1 = (1 - bit1) * 2048
    o2 = c1 + (1 - bit2) * 1024
    o4 = c2 + (1 - bit4) * 512
    oy = c4 + (1 - y_hi) * 256
    halve = [
        remote(DL.at[rows_other, :], CR, sibling),
        remote(AC.at[:, cols_at(o1, 2048)], R1, z_one),
        remote(AC.at[:, cols_at(o2, 1024)], R2, z_two),
        remote(AC.at[:, cols_at(o4, 512)], R3, z_four),
        remote(AC.at[:, cols_at(oy, 256)], R4, across),
    ]
    double = [
        remote(FU.at[rows_mine, cols_at(s, n)], FU.at[rows_mine, cols_at(s, n)], d)
        for s, n, d in ((cy, 256, across), (c4, 512, z_four), (c2, 1024, z_two), (c1, 2048, z_one))
    ]
    double.append(remote(FU.at[rows_mine, :], FU.at[rows_mine, :], sibling))

    def outer_halve(step):
        halve[step].wait_recv()
        if step == 0:
            AC[...] = DL[rows_mine, :] + CR[...]
        else:
            start, width, got = ((c1, 2048, R1), (c2, 1024, R2), (c4, 512, R3), (cy, 256, R4))[step - 1]
            total = AC[:, cols_at(start, width)] + got[...]
            if step < 4:
                AC[:, cols_at(start, width)] = total
            else:
                FU[rows_mine, cols_at(start, width)] = total
        if step < 4:
            halve[step + 1].start()
        else:
            double[0].start()

    def outer_double(step):
        double[step].wait_recv()
        if step < 4:
            double[step + 1].start()

    store_m, store_a = nearby(NM, nm_out), nearby(NA, na_out)

    def outer_update():
        load_m.wait()
        load_a.wait()
        average = FU[...] * f32(1.0 / 32.0)
        momentum = f32(MOMENTUM_RATE) * MO[...] + average
        NM[...] = momentum
        NA[...] = AN[...] - f32(OUTER_RATE) * (average + f32(MOMENTUM_RATE) * momentum)
        store_m.start()
        store_a.start()

    def condition(s, base):
        shift = EM[:, columns(mine[s])].astype(f32)

        def chunk(i, _):
            rows = pl.ds(pl.multiple_of(base + i * 64, 64), 64)
            wide = X[s, rows, :].astype(f32).reshape(4, FRAMES, BLK) + shift[None]
            X[s, rows, :] = wide.reshape(64, BLK).astype(bf16)
            return 0

        lax.fori_loop(0, TOK // 64, chunk, 0)

    def transpose(s, base):
        def chunk(i, _):
            rows = pl.ds(pl.multiple_of(base + i * 128, 128), 128)
            XT[s, :, rows] = X[s, rows, :].T
            return 0

        lax.fori_loop(0, TOK // 128, chunk, 0)

    def project(k, rows):
        total = jnp.dot(X[0, rows, :], WG[k, 0], preferred_element_type=f32)
        for s in range(1, 4):
            total += jnp.dot(X[s, rows, :], WG[k, s], preferred_element_type=f32)
        return total

    def project_other(k):
        KS[k] = project(k, other).astype(bf16)
        kv_send[k].start()

    def project_own(k):
        O[k] = project(k, own)

    def send_w(k):
        for c in load_w[k]:
            c.wait()
        w_right[k].start()
        w_left[k].start()

    def forward_w(k):
        w_right[k].wait_recv()
        w_right2[k].start()
        w_left[k].wait_recv()
        w_left2[k].start()

    def have_w(k):
        w_right2[k].wait_recv()
        w_left2[k].wait_recv()

    def attention(k):
        kv_send[k].wait_recv()
        scale = HEAD_DIM**-0.5
        nt = (((1,), (1,)), ((), ()))

        def block(b, _):
            rows = pl.ds(pl.multiple_of(b * CH, CH), CH)
            kv = (O[k, rows, :] + KR[k, rows, :].astype(f32)).astype(bf16)
            key, value = kv[:, :HEAD_DIM], kv[:, HEAD_DIM:]
            heads = [pl.ds((k * GROUP + j) * HEAD_DIM, HEAD_DIM) for j in range(GROUP)]
            query = jnp.concatenate([QV[rows, h] for h in heads], axis=0)
            up = jnp.concatenate([CV[rows, h] for h in heads], axis=0)
            keep = MK[...] > 0.0
            scores = lax.dot_general(key, query, nt, preferred_element_type=f32)
            scores = jnp.where(keep, scores, f32(-1e30))
            top = jnp.max(scores, axis=0, keepdims=True)
            grown = jnp.exp2((scores - top) * f32(scale * LOG2E))
            probs = grown * (1.0 / jnp.sum(grown, axis=0, keepdims=True))
            prob_grad = lax.dot_general(value, up, nt, preferred_element_type=f32)
            mean = jnp.sum(probs * prob_grad, axis=0, keepdims=True)
            score_grad = (probs * (prob_grad - mean)).astype(bf16)
            G[k, rows, values] = jnp.dot(
                probs.astype(bf16), up, preferred_element_type=f32
            ).astype(bf16)
            G[k, rows, keys] = (
                jnp.dot(score_grad, query, preferred_element_type=f32) * f32(scale)
            ).astype(bf16)
            return 0

        lax.fori_loop(0, TOK // CH, block, 0)
        g_send[k].start()

    def gradient(k):
        g_send[k].wait_recv()
        S3[k] = jnp.dot(XT[3], G[k], preferred_element_type=f32).astype(bf16)
        opp_right[k].start()
        opp_left[k].start()
        to_r = jnp.dot(XT[2], G[k], preferred_element_type=f32)
        T2[k] = to_r[:, :HEAD_DIM]
        S2[k, :, values] = to_r[:, HEAD_DIM:].astype(bf16)
        to_right_v[k].start()
        to_l = jnp.dot(XT[1], G[k], preferred_element_type=f32)
        T1[k] = to_l[:, HEAD_DIM:]
        S1[k, :, keys] = to_l[:, :HEAD_DIM].astype(bf16)
        to_left_k[k].start()
        G0[k] = jnp.dot(XT[0], G[k], preferred_element_type=f32)

    def relay(k):
        opp_right[k].wait_recv()
        S2[k, :, keys] = (T2[k] + OA[k].astype(f32)).astype(bf16)
        to_right_k[k].start()
        opp_left[k].wait_recv()
        S1[k, :, values] = (T1[k] + OB[k].astype(f32)).astype(bf16)
        to_left_v[k].start()

    store_w = [
        [
            nearby(OUT.at[k, :, keys], wg_out.at[0, :, pl.ds(k * HEAD_DIM, HEAD_DIM)]),
            nearby(OUT.at[k, :, values], wg_out.at[0, :, pl.ds((KV_HEADS + k) * HEAD_DIM, HEAD_DIM)]),
        ]
        for k in range(KV_HEADS)
    ]

    def finish(k):
        for c in (to_right_k[k], to_right_v[k], to_left_k[k], to_left_v[k]):
            c.wait_recv()
        OUT[k] = (G0[k] + RL[k].astype(f32) + RR[k].astype(f32)).astype(bf16)
        for c in store_w[k]:
            c.start()

    barrier = pltpu.get_barrier_semaphore()
    peers = (partner, left, right, sibling, z_one, z_two, z_four, across)
    for peer in peers:
        pl.semaphore_signal(barrier, inc=1, device_id=peer, device_id_type=MESH)
    pl.semaphore_wait(barrier, len(peers))

    for c in lat_send:
        c.start()
    send_w(0)
    load_delta.wait()
    halve[0].start()

    t_at = lax.broadcasted_iota(jnp.int32, (CH, CH), 0)
    f_at = lax.broadcasted_iota(jnp.int32, (CH, CH), 1)
    seen = (lax.shift_right_logical(t_at, 4) == lax.shift_right_logical(f_at, 4)) & (t_at <= f_at)
    one = jnp.where(seen, f32(1.0), f32(0.0))
    for j in range(GROUP):
        MK[:, pl.ds(j * CH, CH)] = one

    load_emb.wait()
    for s in range(4):
        load_x[s].wait()
        condition(s, 0)
    outer_halve(0)
    forward_w(0)
    for s in range(4):
        transpose(s, 0)
    outer_halve(1)
    have_w(0)
    project_own(0)
    outer_halve(2)
    for s in range(4):
        lat_send[s].wait_recv()
        condition(s, TOK)
        if s == 1:
            outer_halve(3)
        if s == 2:
            send_w(1)
            outer_halve(4)
    project_other(0)
    send_w(2)
    for s in range(4):
        transpose(s, TOK)
    outer_double(0)
    forward_w(1)
    load_q.wait()
    load_c.wait()
    have_w(1)
    project_other(1)
    project_own(1)
    attention(0)
    send_w(3)
    forward_w(2)
    outer_double(1)
    have_w(2)
    project_other(2)
    project_own(2)
    attention(1)
    forward_w(3)
    gradient(0)
    outer_double(2)
    have_w(3)
    project_other(3)
    project_own(3)
    attention(2)
    gradient(1)
    relay(0)
    outer_double(3)
    attention(3)
    gradient(2)
    relay(1)
    finish(0)
    outer_double(4)
    outer_update()
    gradient(3)
    relay(2)
    finish(1)
    relay(3)
    finish(2)
    finish(3)

    for group in (
        lat_send, w_right, w_left, w_right2, w_left2, kv_send, g_send, opp_right, opp_left,
        to_right_k, to_right_v, to_left_k, to_left_v, halve, double,
    ):
        for c in group:
            c.wait_send()
    for pair in store_w:
        for c in pair:
            c.wait()
    store_m.wait()
    store_a.wait()


def body(
    latent_tokens,
    actions,
    action_table,
    key_value_weight,
    queries,
    output_cotangent,
    outer_delta,
    momentum,
    anchor,
):
    f32, bf16 = jnp.float32, jnp.bfloat16
    one_hot = (actions[0][:, None] == jnp.arange(ACTIONS, dtype=jnp.int32)[None, :]).astype(bf16)
    emb = jnp.dot(one_hot, action_table, preferred_element_type=f32).astype(bf16)
    H = KV_HEADS
    vm = pltpu.VMEM
    scratch = [
        vm((4, 2 * TOK, BLK), bf16),
        vm((4, BLK, 2 * TOK), bf16),
        vm((H, 4, BLK, HW), bf16),
        vm((TOK, 2048), bf16),
        vm((TOK, 2048), bf16),
        vm((FRAMES, 4096), bf16),
        vm((CH, GROUP * CH), f32),
        vm((H, TOK, HW), f32),
        vm((H, TOK, HW), bf16),
        vm((H, TOK, HW), bf16),
        vm((H, 2 * TOK, HW), bf16),
        vm((H, BLK, HW), bf16),
        vm((H, BLK, HW), bf16),
        vm((H, BLK, HW), bf16),
        vm((H, BLK, HEAD_DIM), f32),
        vm((H, BLK, HEAD_DIM), f32),
        vm((H, BLK, HW), f32),
        vm((H, BLK, HEAD_DIM), bf16),
        vm((H, BLK, HEAD_DIM), bf16),
        vm((H, BLK, HW), bf16),
        vm((H, BLK, HW), bf16),
        vm((H, BLK, HW), bf16),
        vm((32, 4096), f32),
        vm((16, 4096), f32),
        vm((16, 4096), f32),
        vm((16, 2048), f32),
        vm((16, 1024), f32),
        vm((16, 512), f32),
        vm((16, 256), f32),
        vm((32, 4096), f32),
        vm((32, 4096), f32),
        vm((32, 4096), f32),
        vm((32, 4096), f32),
        vm((32, 4096), f32),
        pltpu.SemaphoreType.DMA((62,)),
        pltpu.SemaphoreType.DMA((62,)),
        pltpu.SemaphoreType.DMA((32,)),
    ]
    hbm = pl.BlockSpec(memory_space=pl.ANY)
    return pl.pallas_call(
        kernel,
        out_shape=(
            jax.ShapeDtypeStruct((1, BLK, 2 * H * HEAD_DIM), bf16),
            jax.ShapeDtypeStruct((32, 4096), f32),
            jax.ShapeDtypeStruct((32, 4096), f32),
        ),
        in_specs=[hbm] * 8,
        out_specs=(hbm, hbm, hbm),
        scratch_shapes=scratch,
        compiler_params=pltpu.CompilerParams(
            collective_id=0, has_side_effects=True, vmem_limit_bytes=56 * 2**20
        ),
        cost_estimate=pl.CostEstimate(
            flops=10 * 10**9, bytes_accessed=16 * 2**20, transcendentals=10**6
        ),
    )(
        latent_tokens, key_value_weight, emb, queries, output_cotangent, outer_delta, momentum, anchor
    )


def solution(mesh):
    return jax.shard_map(
        body,
        mesh=mesh,
        in_specs=(
            P("rep", "fsdp", None),
            P("rep", None),
            P(),
            P("rep", "fsdp", None),
            P("rep", "fsdp", None),
            P("rep", "fsdp", None),
            P("rep", "fsdp", None),
            P("fsdp", None),
            P("fsdp", None),
        ),
        out_specs=(P("rep", "fsdp", None), P("fsdp", None), P("fsdp", None)),
        check_vma=False,
    )
```

time: 418 us -> 119 us (0.28)
  waiting for transfers between devices: 349 us -> 0 us
  Pallas kernels: 0 us -> 111 us
  matrix products: 31.3 us -> 1.54 us
  between operations: 15.6 us -> 0.67 us
  other arithmetic: 9.09 us -> 0 us
  local copies, waits for them, and re-layouts: 11.1 us -> 4.78 us
    psum x1 -> x0, waiting for transfers between devices: 264 us -> none  [body(): lax.psum(replica_delta.astype(jnp.bfloat16), 'rep').astype(jnp.float32)]
    pallas_call x0 -> x1, Pallas kernels: none -> 111 us  [body(): pl.pallas_call(kernel, out_shape=(jax.ShapeDtypeStruct((1, BLK, 2 * H * H...]
    all_gather x1 -> x0, waiting for transfers between devices: 84 us -> none  [body(): lax.all_gather(weight, 'fsdp', axis=0, tiled=True)]
    dot_general x7 -> x1, matrix products: 31.3 us -> 1.54 us  [body(): jnp.dot(one_hot, action_table, preferred_element_type=f32).astype(bf16)]
    another operation x2 -> x0, local copies, waits for them, and re-layouts: 7.18 us -> none  [the longest x1 4.45 us: attention_grad(): query_rows.reshape(patch_count, FRAMES, KV_HEADS, GROUP, HEAD_DIM)]
    convert_element_type x2 -> x0, other arithmetic: 7.03 us -> none  [the longest x1 5.26 us: condition(): return summed.reshape(token_count, -1).astype(jnp.bfloat16)]
  transfers between devices with their start and end apart: 3 -> 0, of which waited for: 2 -> 0; matrix products, arithmetic and copies ran while one was open for 12% -> 0% of each run, Pallas kernels for 0% -> 0%
where the time goes in v1:
time: 119 us; the launch traced here: 118 us
  Pallas kernels  111 us (93%)
  local copies, waits for them, and re-layouts  4.78 us (4%)
  matrix products  1.54 us (1%)
    pallas_call x1, Pallas kernels, body(): pl.pallas_call(kernel, out_shape=(jax.ShapeDtypeStruct((1, BLK, 2 * H * H...  111 us
    unnamed x9, local copies, waits for them, and re-layouts  4.78 us

profile of v1, /device:TPU:8, one launch (start us, length us, event | category | flops | bytes accessed | tf_op | source)
XLA Modules:
  0.0 118.4 jit_solution(3266849148299736333)
XLA Ops:
  0.6 0.0 copy-start
  0.6 0.8 copy-done
  1.5 1.5 %convolution_convert_fusion.emb = bf16[16,4096]{1,0:T(8,128)(2,1)} fusion(bf16[8,4096]{1,0:T(8,128)(2,1)S(1)} %copy-done, s32[16]{0:T(128)} %bitcast.2), kind=kOutput, calls=%fused_computation | convolution fusion | flops 1114240 | bytes 196672 | tf_op jit(solution)/shard_map/dot_general | solution.py:411
  3.0 111.4 %shard_map.112 = (bf16[1,512,1024]{2,1,0:T(8,128)(2,1)}, f32[32,4096]{1,0:T(8,128)}, f32[32,4096]{1,0:T(8,128)}) custom-call(bf16[1,512,4096]{2,1,0:T(8,128)(2,1)} %lat.1, bf16[1,512,1024]{2,1,0:T(8,128)(2,1)} %w.1, bf16[16,4096]{1,0:T(8,128)(2,1)} %convolution_convert_fusion.emb, bf16[1,512,2048]{2,1,0:T(8,128)(2,1)} %q.1, bf16[1,512,2048]{2,1,0:T(8,128)(2,1)} %cot.1, ...), custom_call_target="tpu_custom_call" | custom-call | flops 10000000000 | bytes 16777216 | tf_op jit(solution)/shard_map/pallas_call | solution.py:454
  114.5 0.0 copy-start.2
  114.5 0.0 copy-start.1
  114.5 2.3 %copy.15 = bf16[1,512,1024]{2,1,0:T(8,128)(2,1)} copy(bf16[1,512,1024]{2,1,0:T(8,128)(2,1)} %get-tuple-element.6) | data formatting | bytes 2097152
  116.8 0.0 copy-done.2
  116.8 0.8 copy.16
  117.6 0.0 copy-done.1
  117.6 0.8 copy.17
Async XLA Ops:
  0.6 0.8 copy-start
  114.5 2.4 %copy-start.2 = (f32[32,4096]{1,0:T(8,128)S(1)}, f32[32,4096]{1,0:T(8,128)}, u32[]{:S(2)}) copy-start(f32[32,4096]{1,0:T(8,128)} %get-tuple-element.7) | copy-start | bytes 1572868
  114.5 3.2 %copy-start.1 = (f32[32,4096]{1,0:T(8,128)S(1)}, f32[32,4096]{1,0:T(8,128)}, u32[]{:S(2)}) copy-start(f32[32,4096]{1,0:T(8,128)} %get-tuple-element.8) | copy-start | bytes 1572868

commit v2 on v1

v2 whole, which is shorter than its diff:
```python
import functools

import jax
import jax.numpy as jnp
from jax import lax
from jax.experimental import pallas as pl
from jax.experimental.pallas import tpu as pltpu
from jax.sharding import PartitionSpec as P

MESH = pl.DeviceIdType.MESH
HEAD_DIM = 128
KV_HEADS = 4
GROUP = 4
ACTIONS = 8
FRAMES = 16
MOMENTUM_RATE = 0.9
OUTER_RATE = 0.7

TOK = 512
BLK = 512
HW = 2 * HEAD_DIM
CH = 128
VIA_B = 192
LOG2E = 1.4426950408889634


def ring_index(core, half, pos):
    even = 4 * half + pos
    row = lax.rem(lax.div(pos + 1, 2), 2)
    odd = 4 * row + half + lax.div(pos, 2) * (3 - 2 * half)
    return even + core * (odd - even)


def kernel(
    lat, act, table, w, q, cot, delta, mom, anc,
    wg_out, nm_out, na_out,
    X, XT, WG, QV, CV, TB, SA, EM, MK, O, KS, KR, G, S3, S2, S1, T2, T1, G0, OA, OB, RA, RB,
    DL, CR, AC, R1, R2, R3, R4, FU, MO, AN,
    send, recv, local,
):
    f32, bf16 = jnp.float32, jnp.bfloat16
    rep = lax.axis_index("rep")
    fsdp = lax.axis_index("fsdp")
    core = lax.rem(rep, 2)
    y_hi = lax.rem(lax.div(rep, 2), 2)
    z = lax.div(rep, 4)
    hi, lo = lax.div(fsdp, 4), lax.rem(fsdp, 4)
    u = lax.div(lo, 2)
    half = hi + core * (lo + u * (3 - 2 * lo) - hi)
    pos = lo + core * (hi + u * (3 - 2 * hi) - lo)
    odd = lax.rem(pos, 2)
    slot_pos = [pos, lax.rem(pos + 3 + 2 * odd, 4), lax.rem(pos + 1 + 2 * odd, 4), lax.rem(pos + 2, 4)]
    mine = [ring_index(core, half, s) for s in slot_pos]
    theirs = [ring_index(core, 1 - half, s) for s in slot_pos]
    to_a, to_b, partner = {"fsdp": mine[1]}, {"fsdp": mine[2]}, {"fsdp": theirs[0]}

    def rep_peer(z_, y_, c_):
        return {"rep": z_ * 4 + y_ * 2 + c_}

    bit1, bit2, bit4 = lax.rem(z, 2), lax.rem(lax.div(z, 2), 2), lax.div(z, 4)
    sibling = rep_peer(z, y_hi, 1 - core)
    z_one = rep_peer(z + 1 - 2 * bit1, y_hi, core)
    z_two = rep_peer(z + 2 - 4 * bit2, y_hi, core)
    z_four = rep_peer(z + 4 - 8 * bit4, y_hi, core)
    across = rep_peer(z, 1 - y_hi, core)

    counts = {"remote": 0, "local": 0}
    loaded = set()

    def remote(src, dst, device):
        n = counts["remote"]
        counts["remote"] = n + 1
        return pltpu.make_async_remote_copy(
            src_ref=src, dst_ref=dst, send_sem=send.at[n], recv_sem=recv.at[n],
            device_id=device, device_id_type=MESH,
        )

    def nearby(src, dst):
        n = counts["local"]
        counts["local"] = n + 1
        return pltpu.make_async_copy(src, dst, local.at[n])

    def columns(i):
        return pl.ds(pl.multiple_of(i * BLK, BLK), BLK)

    keys, values = pl.ds(0, HEAD_DIM), pl.ds(HEAD_DIM, HEAD_DIM)
    own, other = pl.ds(0, TOK), pl.ds(TOK, TOK)
    low, high = pl.ds(0, VIA_B), pl.ds(VIA_B, BLK - VIA_B)

    load_w = [
        [
            nearby(w.at[0, :, pl.ds(k * HEAD_DIM, HEAD_DIM)], WG.at[k, 0, :, keys]),
            nearby(w.at[0, :, pl.ds((KV_HEADS + k) * HEAD_DIM, HEAD_DIM)], WG.at[k, 0, :, values]),
        ]
        for k in range(KV_HEADS)
    ]
    load_x = [nearby(lat.at[0, :, columns(mine[s])], X.at[s, own, :]) for s in range(4)]
    load_act, load_table = nearby(act, SA), nearby(table, TB)
    load_delta = nearby(delta.at[0], DL)
    load_q, load_c = nearby(q.at[0], QV), nearby(cot.at[0], CV)
    load_m, load_a = nearby(mom, MO), nearby(anc, AN)
    for c in load_w[0]:
        c.start()
    load_delta.start()
    load_act.start()
    load_table.start()
    for c in load_x:
        c.start()
    for k in range(1, KV_HEADS):
        for c in load_w[k]:
            c.start()
    for c in (load_q, load_c, load_m, load_a):
        c.start()

    lat_send = [
        remote(lat.at[0, :, columns(theirs[s])], X.at[s, other, :], partner) for s in range(4)
    ]
    w_a = [remote(WG.at[k, 0], WG.at[k, 1], to_a) for k in range(KV_HEADS)]
    w_b = [remote(WG.at[k, 0], WG.at[k, 2], to_b) for k in range(KV_HEADS)]
    w_ab = [remote(WG.at[k, 1, low], WG.at[k, 3, low], to_b) for k in range(KV_HEADS)]
    w_ba = [remote(WG.at[k, 2, high], WG.at[k, 3, high], to_a) for k in range(KV_HEADS)]
    kv_send = [remote(KS.at[k], KR.at[k], partner) for k in range(KV_HEADS)]
    g_send = [remote(G.at[k, own, :], G.at[k, other, :], partner) for k in range(KV_HEADS)]
    opp_a = [remote(S3.at[k, high], OA.at[k], to_a) for k in range(KV_HEADS)]
    opp_b = [remote(S3.at[k, low], OB.at[k], to_b) for k in range(KV_HEADS)]
    sum_b_low = [remote(S2.at[k, low], RB.at[k, low], to_b) for k in range(KV_HEADS)]
    sum_b_high = [remote(S2.at[k, high], RB.at[k, high], to_b) for k in range(KV_HEADS)]
    sum_a_low = [remote(S1.at[k, low], RA.at[k, low], to_a) for k in range(KV_HEADS)]
    sum_a_high = [remote(S1.at[k, high], RA.at[k, high], to_a) for k in range(KV_HEADS)]

    rows_mine = pl.ds(pl.multiple_of(core * 16, 16), 16)
    rows_other = pl.ds(pl.multiple_of((1 - core) * 16, 16), 16)

    def cols_at(start, width):
        return pl.ds(pl.multiple_of(start, 256), width)

    c1 = bit1 * 2048
    c2 = c1 + bit2 * 1024
    c4 = c2 + bit4 * 512
    cy = c4 + y_hi * 256
    o1 = (1 - bit1) * 2048
    o2 = c1 + (1 - bit2) * 1024
    o4 = c2 + (1 - bit4) * 512
    oy = c4 + (1 - y_hi) * 256
    halve = [
        remote(DL.at[rows_other, :], CR, sibling),
        remote(AC.at[:, cols_at(o1, 2048)], R1, z_one),
        remote(AC.at[:, cols_at(o2, 1024)], R2, z_two),
        remote(AC.at[:, cols_at(o4, 512)], R3, z_four),
        remote(AC.at[:, cols_at(oy, 256)], R4, across),
    ]
    double = [
        remote(FU.at[rows_mine, cols_at(s, n)], FU.at[rows_mine, cols_at(s, n)], d)
        for s, n, d in ((cy, 256, across), (c4, 512, z_four), (c2, 1024, z_two), (c1, 2048, z_one))
    ]
    double.append(remote(FU.at[rows_mine, :], FU.at[rows_mine, :], sibling))

    def outer_halve(step):
        halve[step].wait_recv()
        if step == 0:
            AC[...] = DL[rows_mine, :] + CR[...]
        else:
            start, width, got = ((c1, 2048, R1), (c2, 1024, R2), (c4, 512, R3), (cy, 256, R4))[step - 1]
            total = AC[:, cols_at(start, width)] + got[...]
            if step < 4:
                AC[:, cols_at(start, width)] = total
            else:
                FU[rows_mine, cols_at(start, width)] = total
        if step < 4:
            halve[step + 1].start()
        else:
            double[0].start()

    def outer_double(step):
        double[step].wait_recv()
        if step < 4:
            double[step + 1].start()

    def outer_update():
        load_m.wait()
        load_a.wait()
        average = FU[...] * f32(1.0 / 32.0)
        momentum = f32(MOMENTUM_RATE) * MO[...] + average
        nm_out[...] = momentum
        na_out[...] = AN[...] - f32(OUTER_RATE) * (average + f32(MOMENTUM_RATE) * momentum)

    def build_mask():
        t_at = lax.broadcasted_iota(jnp.int32, (CH, CH), 0)
        f_at = lax.broadcasted_iota(jnp.int32, (CH, CH), 1)
        seen = (lax.shift_right_logical(t_at, 4) == lax.shift_right_logical(f_at, 4)) & (t_at <= f_at)
        one = jnp.where(seen, f32(1.0), f32(0.0))
        for j in range(GROUP):
            MK[:, pl.ds(j * CH, CH)] = one

    def embed():
        load_act.wait()
        load_table.wait()
        frame = lax.broadcasted_iota(jnp.int32, (FRAMES, BLK), 0)
        chosen = jnp.zeros((FRAMES, BLK), jnp.int32)
        for f in range(FRAMES):
            chosen = jnp.where(frame == f, SA[0, f], chosen)
        for s in range(4):
            rows = TB[:, columns(mine[s])].astype(f32)
            shift = jnp.zeros((FRAMES, BLK), f32)
            for a in range(ACTIONS):
                shift = jnp.where(chosen == a, rows[a : a + 1, :], shift)
            EM[s] = shift

    def condition(s, base):
        shift = EM[s]

        def chunk(i, _):
            rows = pl.ds(pl.multiple_of(base + i * 64, 64), 64)
            wide = X[s, rows, :].astype(f32).reshape(4, FRAMES, BLK) + shift[None]
            X[s, rows, :] = wide.reshape(64, BLK).astype(bf16)
            return 0

        lax.fori_loop(0, TOK // 64, chunk, 0)

    def transpose(s, base):
        def chunk(i, _):
            rows = pl.ds(pl.multiple_of(base + i * 128, 128), 128)
            XT[s, :, rows] = X[s, rows, :].T
            return 0

        lax.fori_loop(0, TOK // 128, chunk, 0)

    def project(k, rows):
        total = jnp.dot(X[0, rows, :], WG[k, 0], preferred_element_type=f32)
        for s in range(1, 4):
            total += jnp.dot(X[s, rows, :], WG[k, s], preferred_element_type=f32)
        return total

    def project_other(k):
        KS[k] = project(k, other).astype(bf16)
        kv_send[k].start()

    def condition_own(s):
        load_x[s].wait()
        condition(s, 0)

    def condition_other(s):
        lat_send[s].wait_recv()
        condition(s, TOK)

    def project_first(s):
        part = jnp.dot(X[s, other, :], WG[0, s], preferred_element_type=f32)
        if s == 0:
            G0[0] = part
        elif s < 3:
            G0[0] += part
        else:
            KS[0] = (G0[0] + part).astype(bf16)
            kv_send[0].start()

    def project_own(k):
        O[k] = project(k, own)

    def send_w(k, copy):
        if k not in loaded:
            loaded.add(k)
            for c in load_w[k]:
                c.wait()
        copy.start()

    def forward_ab(k):
        w_a[k].wait_recv()
        w_ab[k].start()

    def forward_ba(k):
        w_b[k].wait_recv()
        w_ba[k].start()

    def have_w(k):
        w_ab[k].wait_recv()
        w_ba[k].wait_recv()

    def attention(k):
        kv_send[k].wait_recv()
        scale = HEAD_DIM**-0.5
        nt = (((1,), (1,)), ((), ()))

        def block(b, _):
            rows = pl.ds(pl.multiple_of(b * CH, CH), CH)
            kv = (O[k, rows, :] + KR[k, rows, :].astype(f32)).astype(bf16)
            key, value = kv[:, :HEAD_DIM], kv[:, HEAD_DIM:]
            heads = [pl.ds((k * GROUP + j) * HEAD_DIM, HEAD_DIM) for j in range(GROUP)]
            query = jnp.concatenate([QV[rows, h] for h in heads], axis=0)
            up = jnp.concatenate([CV[rows, h] for h in heads], axis=0)
            keep = MK[...] > 0.0
            scores = lax.dot_general(key, query, nt, preferred_element_type=f32)
            scores = jnp.where(keep, scores, f32(-1e30))
            top = jnp.max(scores, axis=0, keepdims=True)
            grown = jnp.exp2((scores - top) * f32(scale * LOG2E))
            probs = grown * (1.0 / jnp.sum(grown, axis=0, keepdims=True))
            prob_grad = lax.dot_general(value, up, nt, preferred_element_type=f32)
            mean = jnp.sum(probs * prob_grad, axis=0, keepdims=True)
            score_grad = (probs * (prob_grad - mean)).astype(bf16)
            G[k, rows, values] = jnp.dot(
                probs.astype(bf16), up, preferred_element_type=f32
            ).astype(bf16)
            G[k, rows, keys] = (
                jnp.dot(score_grad, query, preferred_element_type=f32) * f32(scale)
            ).astype(bf16)
            return 0

        lax.fori_loop(0, TOK // CH, block, 0, unroll=4)
        g_send[k].start()

    def gradient_opposite(k):
        g_send[k].wait_recv()
        S3[k] = jnp.dot(XT[3], G[k], preferred_element_type=f32).astype(bf16)
        opp_a[k].start()
        opp_b[k].start()

    def gradient_a(k):
        part = jnp.dot(XT[1], G[k], preferred_element_type=f32)
        T1[k] = part[:VIA_B]
        S1[k, high] = part[VIA_B:].astype(bf16)
        sum_a_high[k].start()

    def gradient_b(k):
        part = jnp.dot(XT[2], G[k], preferred_element_type=f32)
        T2[k] = part[VIA_B:]
        S2[k, low] = part[:VIA_B].astype(bf16)
        sum_b_low[k].start()

    def gradient_own(k):
        G0[k] = jnp.dot(XT[0], G[k], preferred_element_type=f32)

    def relay_to_b(k):
        opp_a[k].wait_recv()
        S2[k, high] = (T2[k] + OA[k].astype(f32)).astype(bf16)
        sum_b_high[k].start()

    def relay_to_a(k):
        opp_b[k].wait_recv()
        S1[k, low] = (T1[k] + OB[k].astype(f32)).astype(bf16)
        sum_a_low[k].start()

    def finish(k):
        for c in (sum_a_low[k], sum_a_high[k], sum_b_low[k], sum_b_high[k]):
            c.wait_recv()
        total = (G0[k] + RA[k].astype(f32) + RB[k].astype(f32)).astype(bf16)
        wg_out[0, :, pl.ds(k * HEAD_DIM, HEAD_DIM)] = total[:, :HEAD_DIM]
        wg_out[0, :, pl.ds((KV_HEADS + k) * HEAD_DIM, HEAD_DIM)] = total[:, HEAD_DIM:]

    barrier = pltpu.get_barrier_semaphore()
    peers = (partner, to_a, to_b, sibling, z_one, z_two, z_four, across)
    for peer in peers:
        pl.semaphore_signal(barrier, inc=1, device_id=peer, device_id_type=MESH)
    pl.semaphore_wait(barrier, len(peers))

    lat_send[0].start()
    send_w(2, w_a[2])
    lat_send[3].start()
    send_w(1, w_a[1])
    send_w(0, w_b[0])
    load_delta.wait()
    halve[0].start()
    send_w(1, w_b[1])
    embed()
    forward_ab(2)
    condition_own(2)
    forward_ab(1)
    lat_send[2].start()
    send_w(3, w_a[3])
    send_w(0, w_a[0])
    forward_ba(1)
    outer_halve(0)
    outer_halve(1)
    outer_halve(2)
    condition_own(3)
    condition_own(1)
    lat_send[1].start()
    condition_own(0)
    have_w(1)
    condition_other(2)
    send_w(3, w_b[3])
    transpose(2, 0)
    outer_halve(3)
    transpose(3, 0)
    condition_other(3)
    forward_ab(0)
    build_mask()
    forward_ba(0)
    transpose(2, TOK)
    condition_other(0)
    outer_halve(4)
    condition_other(1)
    project_other(1)
    transpose(0, 0)
    transpose(3, TOK)
    project_own(1)
    have_w(0)
    send_w(2, w_b[2])
    transpose(0, TOK)
    forward_ab(3)
    forward_ba(3)
    load_q.wait()
    load_c.wait()
    attention(1)
    forward_ba(2)
    have_w(3)
    project_other(3)
    transpose(1, TOK)
    project_first(0)
    project_first(1)
    project_first(2)
    project_own(3)
    outer_double(0)
    transpose(1, 0)
    project_first(3)
    gradient_opposite(1)
    gradient_own(1)
    have_w(2)
    project_own(0)
    gradient_a(1)
    attention(3)
    outer_double(1)
    relay_to_a(1)
    attention(0)
    gradient_b(1)
    gradient_opposite(3)
    project_other(2)
    project_own(2)
    outer_double(2)
    gradient_a(3)
    gradient_b(3)
    outer_double(3)
    gradient_opposite(0)
    gradient_a(0)
    relay_to_b(3)
    relay_to_a(3)
    attention(2)
    relay_to_a(0)
    gradient_own(0)
    gradient_opposite(2)
    gradient_own(3)
    gradient_b(0)
    outer_double(4)
    relay_to_b(1)
    outer_update()
    relay_to_b(0)
    gradient_a(2)
    gradient_b(2)
    finish(0)
    finish(3)
    gradient_own(2)
    relay_to_b(2)
    relay_to_a(2)
    finish(1)
    finish(2)

    for group in (
        lat_send, w_a, w_b, w_ab, w_ba, kv_send, g_send, opp_a, opp_b,
        sum_a_low, sum_a_high, sum_b_low, sum_b_high, halve, double,
    ):
        for c in group:
            c.wait_send()


def body(
    latent_tokens,
    actions,
    action_table,
    key_value_weight,
    queries,
    output_cotangent,
    outer_delta,
    momentum,
    anchor,
):
    f32, bf16 = jnp.float32, jnp.bfloat16
    H = KV_HEADS
    vm = pltpu.VMEM
    scratch = [
        vm((4, 2 * TOK, BLK), bf16),
        vm((4, BLK, 2 * TOK), bf16),
        vm((H, 4, BLK, HW), bf16),
        vm((TOK, 2048), bf16),
        vm((TOK, 2048), bf16),
        vm((ACTIONS, 4096), bf16),
        pltpu.SMEM((1, FRAMES), jnp.int32),
        vm((4, FRAMES, BLK), f32),
        vm((CH, GROUP * CH), f32),
        vm((H, TOK, HW), f32),
        vm((H, TOK, HW), bf16),
        vm((H, TOK, HW), bf16),
        vm((H, 2 * TOK, HW), bf16),
        vm((H, BLK, HW), bf16),
        vm((H, BLK, HW), bf16),
        vm((H, BLK, HW), bf16),
        vm((H, BLK - VIA_B, HW), f32),
        vm((H, VIA_B, HW), f32),
        vm((H, BLK, HW), f32),
        vm((H, BLK - VIA_B, HW), bf16),
        vm((H, VIA_B, HW), bf16),
        vm((H, BLK, HW), bf16),
        vm((H, BLK, HW), bf16),
        vm((32, 4096), f32),
        vm((16, 4096), f32),
        vm((16, 4096), f32),
        vm((16, 2048), f32),
        vm((16, 1024), f32),
        vm((16, 512), f32),
        vm((16, 256), f32),
        vm((32, 4096), f32),
        vm((32, 4096), f32),
        vm((32, 4096), f32),
        pltpu.SemaphoreType.DMA((62,)),
        pltpu.SemaphoreType.DMA((62,)),
        pltpu.SemaphoreType.DMA((24,)),
    ]
    hbm = pl.BlockSpec(memory_space=pl.ANY)
    vmem = pl.BlockSpec(memory_space=pltpu.VMEM)
    return pl.pallas_call(
        kernel,
        out_shape=(
            vm((1, BLK, 2 * H * HEAD_DIM), bf16),
            vm((32, 4096), f32),
            vm((32, 4096), f32),
        ),
        in_specs=[hbm] * 9,
        out_specs=(vmem, vmem, vmem),
        scratch_shapes=scratch,
        compiler_params=pltpu.CompilerParams(
            collective_id=0, has_side_effects=True, vmem_limit_bytes=56 * 2**20
        ),
        cost_estimate=pl.CostEstimate(
            flops=10 * 10**9, bytes_accessed=16 * 2**20, transcendentals=10**6
        ),
    )(
        latent_tokens, actions, action_table, key_value_weight, queries, output_cotangent,
        outer_delta, momentum, anchor,
    )


def solution(mesh):
    return jax.shard_map(
        body,
        mesh=mesh,
        in_specs=(
            P("rep", "fsdp", None),
            P("rep", None),
            P(),
            P("rep", "fsdp", None),
            P("rep", "fsdp", None),
            P("rep", "fsdp", None),
            P("rep", "fsdp", None),
            P("fsdp", None),
            P("fsdp", None),
        ),
        out_specs=(P("rep", "fsdp", None), P("fsdp", None), P("fsdp", None)),
        check_vma=False,
    )
```

time: 119 us -> 112 us (0.941)
  local copies, waits for them, and re-layouts: 4.78 us -> 2.56 us
  Pallas kernels: 111 us -> 109 us
  matrix products: 1.54 us -> 0 us
    pallas_call x1, Pallas kernels: 111 us -> 109 us  [body(): pl.pallas_call(kernel, out_shape=(vm((1, BLK, 2 * H * HEAD_DIM), bf16), v...]
    unnamed x9 -> x3, local copies, waits for them, and re-layouts: 4.78 us -> 2.56 us
    dot_general x1 -> x0, matrix products: 1.54 us -> none  [body(): jnp.dot(one_hot, action_table, preferred_element_type=f32).astype(bf16)]
where the time goes in v2:
time: 112 us
  Pallas kernels  109 us (97%)
  local copies, waits for them, and re-layouts  2.56 us (2%)
    pallas_call x1, Pallas kernels, body(): pl.pallas_call(kernel, out_shape=(vm((1, BLK, 2 * H * HEAD_DIM), bf16), v...  109 us
    unnamed x3, local copies, waits for them, and re-layouts  2.56 us

profile of v2, /device:TPU:8, one launch (start us, length us, event | category | flops | bytes accessed | tf_op | source)
XLA Modules:
  0.0 111.9 jit_solution(514693639157302554)
XLA Ops:
  0.6 108.7 %shard_map.112 = (bf16[1,512,1024]{2,1,0:T(8,128)(2,1)S(1)}, f32[32,4096]{1,0:T(8,128)S(1)}, f32[32,4096]{1,0:T(8,128)S(1)}) custom-call(bf16[1,512,4096]{2,1,0:T(8,128)(2,1)} %lat.1, s32[1,16]{1,0:T(1,128)} %act.1, bf16[8,4096]{1,0:T(8,128)(2,1)} %table.1, bf16[1,512,1024]{2,1,0:T(8,128)(2,1)} %w.1, bf16[1,512,2048]{2,1,0:T(8,128)(2,1)} %q.1, ...), custom_call_target="tpu_custom_call" | custom-call | flops 10000000000 | bytes 16777216 | tf_op jit(solution)/shard_map/pallas_call | solution.py:517
  109.3 1.0 copy.15
  110.3 0.8 copy.16
  111.1 0.8 copy.17

commit v3 on v2

--- a/solution.py
+++ b/solution.py
@@ -20,7 +20,7 @@
 BLK = 512
 HW = 2 * HEAD_DIM
 CH = 128
-VIA_B = 192
+VIA_B = 336
 LOG2E = 1.4426950408889634
 
 
@@ -117,8 +117,7 @@
     ]
     w_a = [remote(WG.at[k, 0], WG.at[k, 1], to_a) for k in range(KV_HEADS)]
     w_b = [remote(WG.at[k, 0], WG.at[k, 2], to_b) for k in range(KV_HEADS)]
-    w_ab = [remote(WG.at[k, 1, low], WG.at[k, 3, low], to_b) for k in range(KV_HEADS)]
-    w_ba = [remote(WG.at[k, 2, high], WG.at[k, 3, high], to_a) for k in range(KV_HEADS)]
+    w_ba = [remote(WG.at[k, 2], WG.at[k, 3], to_a) for k in range(KV_HEADS)]
     kv_send = [remote(KS.at[k], KR.at[k], partner) for k in range(KV_HEADS)]
     g_send = [remote(G.at[k, own, :], G.at[k, other, :], partner) for k in range(KV_HEADS)]
     opp_a = [remote(S3.at[k, high], OA.at[k], to_a) for k in range(KV_HEADS)]
@@ -155,11 +154,29 @@
     ]
     double.append(remote(FU.at[rows_mine, :], FU.at[rows_mine, :], sibling))
 
+    bits = [None, bit1, bit2, bit4, y_hi]
+
+    def outer_offer(step):
+        @pl.when(bits[step] == 1)
+        def _():
+            halve[step].start()
+
+    def outer_answer(step):
+        @pl.when(bits[step] == 0)
+        def _():
+            halve[step].wait_recv()
+            halve[step].start()
+
     def outer_halve(step):
-        halve[step].wait_recv()
         if step == 0:
+            halve[0].wait_recv()
             AC[...] = DL[rows_mine, :] + CR[...]
         else:
+
+            @pl.when(bits[step] == 1)
+            def _():
+                halve[step].wait_recv()
+
             start, width, got = ((c1, 2048, R1), (c2, 1024, R2), (c4, 512, R3), (cy, 256, R4))[step - 1]
             total = AC[:, cols_at(start, width)] + got[...]
             if step < 4:
@@ -167,7 +184,7 @@
             else:
                 FU[rows_mine, cols_at(start, width)] = total
         if step < 4:
-            halve[step + 1].start()
+            outer_offer(step + 1)
         else:
             double[0].start()
 
@@ -263,16 +280,12 @@
                 c.wait()
         copy.start()
 
-    def forward_ab(k):
-        w_a[k].wait_recv()
-        w_ab[k].start()
-
     def forward_ba(k):
         w_b[k].wait_recv()
         w_ba[k].start()
 
     def have_w(k):
-        w_ab[k].wait_recv()
+        w_a[k].wait_recv()
         w_ba[k].wait_recv()
 
     def attention(k):
@@ -346,114 +359,120 @@
         wg_out[0, :, pl.ds((KV_HEADS + k) * HEAD_DIM, HEAD_DIM)] = total[:, HEAD_DIM:]
 
     barrier = pltpu.get_barrier_semaphore()
-    peers = (partner, to_a, to_b, sibling, z_one, z_two, z_four, across)
+    peers = (partner, to_a, to_b, sibling)
     for peer in peers:
         pl.semaphore_signal(barrier, inc=1, device_id=peer, device_id_type=MESH)
-    pl.semaphore_wait(barrier, len(peers))
-
-    lat_send[0].start()
+    for bit, peer in ((bit1, z_one), (bit2, z_two), (bit4, z_four), (y_hi, across)):
+
+        @pl.when(bit == 0)
+        def _():
+            pl.semaphore_signal(barrier, inc=1, device_id=peer, device_id_type=MESH)
+
+    pl.semaphore_wait(barrier, len(peers) + bit1 + bit2 + bit4 + y_hi)
+
+    send_w(1, w_b[1])
+    send_w(1, w_a[1])
+    embed()
+    lat_send[3].start()
     send_w(2, w_a[2])
-    lat_send[3].start()
-    send_w(1, w_a[1])
-    send_w(0, w_b[0])
     load_delta.wait()
     halve[0].start()
-    send_w(1, w_b[1])
-    embed()
-    forward_ab(2)
+    outer_halve(0)
+    lat_send[0].start()
+    build_mask()
+    lat_send[1].start()
+    outer_answer(1)
+    send_w(2, w_b[2])
+    forward_ba(1)
+    outer_halve(1)
+    condition_own(3)
+    lat_send[2].start()
+    outer_answer(2)
+    condition_own(0)
+    send_w(3, w_a[3])
+    forward_ba(2)
+    outer_halve(2)
+    outer_answer(3)
     condition_own(2)
-    forward_ab(1)
-    lat_send[2].start()
-    send_w(3, w_a[3])
+    send_w(0, w_b[0])
+    condition_own(1)
+    transpose(1, 0)
     send_w(0, w_a[0])
-    forward_ba(1)
-    outer_halve(0)
-    outer_halve(1)
-    outer_halve(2)
-    condition_own(3)
-    condition_own(1)
-    lat_send[1].start()
-    condition_own(0)
+    send_w(3, w_b[3])
     have_w(1)
+    transpose(0, 0)
+    condition_other(3)
+    condition_other(1)
+    outer_halve(3)
+    transpose(2, 0)
     condition_other(2)
-    send_w(3, w_b[3])
-    transpose(2, 0)
-    outer_halve(3)
-    transpose(3, 0)
-    condition_other(3)
-    forward_ab(0)
-    build_mask()
+    condition_other(0)
+    have_w(2)
+    project_own(2)
+    transpose(3, TOK)
+    project_other(2)
+    outer_answer(4)
     forward_ba(0)
-    transpose(2, TOK)
-    condition_other(0)
-    outer_halve(4)
-    condition_other(1)
+    project_own(1)
     project_other(1)
-    transpose(0, 0)
-    transpose(3, TOK)
-    project_own(1)
-    have_w(0)
-    send_w(2, w_b[2])
-    transpose(0, TOK)
-    forward_ab(3)
-    forward_ba(3)
     load_q.wait()
     load_c.wait()
+    attention(2)
+    forward_ba(3)
+    transpose(3, 0)
+    outer_halve(4)
+    have_w(0)
+    project_first(0)
     attention(1)
-    forward_ba(2)
+    project_first(1)
+    gradient_opposite(2)
+    transpose(1, TOK)
+    project_first(2)
+    project_first(3)
+    gradient_a(2)
+    project_own(0)
     have_w(3)
     project_other(3)
-    transpose(1, TOK)
-    project_first(0)
-    project_first(1)
-    project_first(2)
+    gradient_opposite(1)
     project_own(3)
+    transpose(2, TOK)
+    gradient_a(1)
+    relay_to_a(2)
     outer_double(0)
-    transpose(1, 0)
-    project_first(3)
-    gradient_opposite(1)
+    attention(0)
+    transpose(0, TOK)
+    relay_to_a(1)
+    attention(3)
+    gradient_opposite(0)
+    gradient_b(2)
+    outer_double(1)
+    gradient_a(0)
+    gradient_own(0)
+    gradient_opposite(3)
+    gradient_a(3)
+    gradient_b(0)
+    relay_to_b(2)
+    gradient_b(3)
+    outer_double(2)
+    gradient_own(2)
+    relay_to_a(0)
+    relay_to_a(3)
+    relay_to_b(0)
+    gradient_b(1)
+    gradient_own(3)
+    relay_to_b(1)
+    outer_double(3)
+    finish(2)
+    outer_double(4)
+    outer_update()
+    finish(0)
     gradient_own(1)
-    have_w(2)
-    project_own(0)
-    gradient_a(1)
-    attention(3)
-    outer_double(1)
-    relay_to_a(1)
-    attention(0)
-    gradient_b(1)
-    gradient_opposite(3)
-    project_other(2)
-    project_own(2)
-    outer_double(2)
-    gradient_a(3)
-    gradient_b(3)
-    outer_double(3)
-    gradient_opposite(0)
-    gradient_a(0)
     relay_to_b(3)
-    relay_to_a(3)
-    attention(2)
-    relay_to_a(0)
-    gradient_own(0)
-    gradient_opposite(2)
-    gradient_own(3)
-    gradient_b(0)
-    outer_double(4)
-    relay_to_b(1)
-    outer_update()
-    relay_to_b(0)
-    gradient_a(2)
-    gradient_b(2)
-    finish(0)
+    finish(1)
     finish(3)
-    gradient_own(2)
-    relay_to_b(2)
-    relay_to_a(2)
-    finish(1)
-    finish(2)
 
     for group in (
-        lat_send, w_a, w_b, w_ab, w_ba, kv_send, g_send, opp_a, opp_b,
+        lat_send, w_a, w_b, w_ba, kv_send, g_send, opp_a, opp_b,
         sum_a_low, sum_a_high, sum_b_low, sum_b_high, halve, double,
     ):
         for c in group:
@@ -508,8 +527,8 @@
         vm((32, 4096), f32),
         vm((32, 4096), f32),
         vm((32, 4096), f32),
-        pltpu.SemaphoreType.DMA((62,)),
-        pltpu.SemaphoreType.DMA((62,)),
+        pltpu.SemaphoreType.DMA((58,)),
+        pltpu.SemaphoreType.DMA((58,)),
         pltpu.SemaphoreType.DMA((24,)),
     ]
     hbm = pl.BlockSpec(memory_space=pl.ANY)

time: 112 us -> 97.1 us (0.87); the launches traced: 112 us -> 95.7 us
  Pallas kernels: 109 us -> 92.5 us
    pallas_call x1, Pallas kernels: 109 us -> 92.5 us  [body(): pl.pallas_call(kernel, out_shape=(vm((1, BLK, 2 * H * HEAD_DIM), bf16), v...]
where the time goes in v3:
time: 97.1 us; the launch traced here: 95.7 us
  Pallas kernels  92.5 us (95%)
  local copies, waits for them, and re-layouts  2.56 us (3%)
    pallas_call x1, Pallas kernels, body(): pl.pallas_call(kernel, out_shape=(vm((1, BLK, 2 * H * HEAD_DIM), bf16), v...  92.5 us
    unnamed x3, local copies, waits for them, and re-layouts  2.56 us

profile of v3, /device:TPU:8, one launch (start us, length us, event | category | flops | bytes accessed | tf_op | source)
XLA Modules:
  0.0 95.7 jit_solution(2105447309958365345)
XLA Ops:
  0.6 92.5 %shard_map.112 = (bf16[1,512,1024]{2,1,0:T(8,128)(2,1)S(1)}, f32[32,4096]{1,0:T(8,128)S(1)}, f32[32,4096]{1,0:T(8,128)S(1)}) custom-call(bf16[1,512,4096]{2,1,0:T(8,128)(2,1)} %lat.1, s32[1,16]{1,0:T(1,128)} %act.1, bf16[8,4096]{1,0:T(8,128)(2,1)} %table.1, bf16[1,512,1024]{2,1,0:T(8,128)(2,1)} %w.1, bf16[1,512,2048]{2,1,0:T(8,128)(2,1)} %q.1, ...), custom_call_target="tpu_custom_call" | custom-call | flops 10000000000 | bytes 16777216 | tf_op jit(solution)/shard_map/pallas_call | solution.py:536
  93.2 1.0 %copy.15 = bf16[1,512,1024]{2,1,0:T(8,128)(2,1)} copy(bf16[1,512,1024]{2,1,0:T(8,128)(2,1)S(1)} %get-tuple-element.3) | data formatting | bytes 2097152
  94.1 0.8 copy.16
  94.9 0.8 copy.17

commit v4 on v3

--- a/solution.py
+++ b/solution.py
@@ -99,18 +99,12 @@
     load_delta = nearby(delta.at[0], DL)
     load_q, load_c = nearby(q.at[0], QV), nearby(cot.at[0], CV)
     load_m, load_a = nearby(mom, MO), nearby(anc, AN)
-    for c in load_w[0]:
-        c.start()
+    for k in (1, 2):
+        for c in load_w[k]:
+            c.start()
     load_delta.start()
     load_act.start()
     load_table.start()
-    for c in load_x:
-        c.start()
-    for k in range(1, KV_HEADS):
-        for c in load_w[k]:
-            c.start()
-    for c in (load_q, load_c, load_m, load_a):
-        c.start()
 
     lat_send = [
         remote(lat.at[0, :, columns(theirs[s])], X.at[s, other, :], partner) for s in range(4)
@@ -377,6 +371,11 @@
     send_w(2, w_a[2])
     load_delta.wait()
     halve[0].start()
+    for c in load_x:
+        c.start()
+    for k in (0, 3):
+        for c in load_w[k]:
+            c.start()
     outer_halve(0)
     lat_send[0].start()
     build_mask()
@@ -384,6 +383,8 @@
     outer_answer(1)
     send_w(2, w_b[2])
     forward_ba(1)
+    for c in (load_q, load_c):
+        c.start()
     outer_halve(1)
     condition_own(3)
     lat_send[2].start()
@@ -391,6 +392,8 @@
     condition_own(0)
     send_w(3, w_a[3])
     forward_ba(2)
+    for c in (load_m, load_a):
+        c.start()
     outer_halve(2)
     outer_answer(3)
     condition_own(2)

time: 97.1 us -> 96 us (0.989)
  no operation moved by 1% of the time
where the time goes in v4:
time: 96 us; the launch traced here: 95.3 us
  Pallas kernels  92.1 us (96%)
  local copies, waits for them, and re-layouts  2.56 us (3%)
    pallas_call x1, Pallas kernels, body(): pl.pallas_call(kernel, out_shape=(vm((1, BLK, 2 * H * HEAD_DIM), bf16), v...  92.1 us
    unnamed x3, local copies, waits for them, and re-layouts  2.56 us

profile of v4, /device:TPU:8, one launch (start us, length us, event | category | flops | bytes accessed | tf_op | source)
XLA Modules:
  0.0 95.3 jit_solution(11655551335216717589)
XLA Ops:
  0.6 92.1 %shard_map.112 = (bf16[1,512,1024]{2,1,0:T(8,128)(2,1)S(1)}, f32[32,4096]{1,0:T(8,128)S(1)}, f32[32,4096]{1,0:T(8,128)S(1)}) custom-call(bf16[1,512,4096]{2,1,0:T(8,128)(2,1)} %lat.1, s32[1,16]{1,0:T(1,128)} %act.1, bf16[8,4096]{1,0:T(8,128)(2,1)} %table.1, bf16[1,512,1024]{2,1,0:T(8,128)(2,1)} %w.1, bf16[1,512,2048]{2,1,0:T(8,128)(2,1)} %q.1, ...), custom_call_target="tpu_custom_call" | custom-call | flops 10000000000 | bytes 16777216 | tf_op jit(solution)/shard_map/pallas_call | solution.py:539
  92.7 1.0 %copy.15 = bf16[1,512,1024]{2,1,0:T(8,128)(2,1)} copy(bf16[1,512,1024]{2,1,0:T(8,128)(2,1)S(1)} %get-tuple-element.3) | data formatting | bytes 2097152
  93.7 0.8 copy.16
  94.5 0.8 copy.17

commit v5 on v4

--- a/solution.py
+++ b/solution.py
@@ -380,28 +380,28 @@
     lat_send[0].start()
     build_mask()
     lat_send[1].start()
-    outer_answer(1)
     send_w(2, w_b[2])
+    condition_own(3)
     forward_ba(1)
     for c in (load_q, load_c):
         c.start()
+    outer_answer(1)
     outer_halve(1)
-    condition_own(3)
     lat_send[2].start()
-    outer_answer(2)
     condition_own(0)
     send_w(3, w_a[3])
     forward_ba(2)
     for c in (load_m, load_a):
         c.start()
+    outer_answer(2)
     outer_halve(2)
-    outer_answer(3)
     condition_own(2)
     send_w(0, w_b[0])
     condition_own(1)
     transpose(1, 0)
     send_w(0, w_a[0])
     send_w(3, w_b[3])
+    outer_answer(3)
     have_w(1)
     transpose(0, 0)
     condition_other(3)

time: 96 us -> 94.9 us (0.989)
  no operation moved by 1% of the time
where the time goes in v5:
time: 94.9 us; the launch traced here: 94.7 us
  Pallas kernels  91.5 us (96%)
  local copies, waits for them, and re-layouts  2.56 us (3%)
    pallas_call x1, Pallas kernels, body(): pl.pallas_call(kernel, out_shape=(vm((1, BLK, 2 * H * HEAD_DIM), bf16), v...  91.5 us
    unnamed x3, local copies, waits for them, and re-layouts  2.56 us

profile of v5, /device:TPU:8, one launch (start us, length us, event | category | flops | bytes accessed | tf_op | source)
XLA Modules:
  0.0 94.7 jit_solution(1600071651926973628)
XLA Ops:
  0.6 91.5 %shard_map.112 = (bf16[1,512,1024]{2,1,0:T(8,128)(2,1)S(1)}, f32[32,4096]{1,0:T(8,128)S(1)}, f32[32,4096]{1,0:T(8,128)S(1)}) custom-call(bf16[1,512,4096]{2,1,0:T(8,128)(2,1)} %lat.1, s32[1,16]{1,0:T(1,128)} %act.1, bf16[8,4096]{1,0:T(8,128)(2,1)} %table.1, bf16[1,512,1024]{2,1,0:T(8,128)(2,1)} %w.1, bf16[1,512,2048]{2,1,0:T(8,128)(2,1)} %q.1, ...), custom_call_target="tpu_custom_call" | custom-call | flops 10000000000 | bytes 16777216 | tf_op jit(solution)/shard_map/pallas_call | solution.py:539
  92.2 1.0 %copy.15 = bf16[1,512,1024]{2,1,0:T(8,128)(2,1)} copy(bf16[1,512,1024]{2,1,0:T(8,128)(2,1)S(1)} %get-tuple-element.3) | data formatting | bytes 2097152
  93.1 0.8 copy.16
  93.9 0.8 copy.17
